TPU v7x, 512 devices: a whole 4x4x16 slice. The times are simulated.
512 devices in a mesh: ctx: 32 (over y, x, core), exp: 16 (over z).
Axes of the slice: x: 4, y: 4, z: 16, core: 2. Of those that a mesh axis runs over, the one named last changes fastest.
Arguments:
- queries: bfloat16 [2048, 64, 576], P('ctx', 'exp'), may hold values from -5 to 5
- out_grad: bfloat16 [2048, 64, 512], P('ctx', 'exp'), may hold values from -3 to 3
- attn_out: bfloat16 [2048, 64, 512], P('ctx', 'exp'), may hold values from -5 to 5
- log_totals: bfloat16 [64, 2048], P('exp', 'ctx')
- latents: bfloat16 [2048, 576], P('ctx'), may hold values from -5 to 5
- moe_inputs: bfloat16 [2048, 7168], P('exp', 'ctx'), may hold values from -6 to 6
- moe_grad: bfloat16 [2048, 7168], P('exp', 'ctx'), may hold values from -6 to 6
- expert_ids: int32 [2048, 1], P('exp'), may hold values from 0 to 15; in each aligned block of 128 rows (0 to 127, 128 to 255, ...) at most 16 rows name the same one
- gate_weight: bfloat16 [16, 7168, 1024], P('exp', 'ctx'), may hold values from -0.0625 to 0.0625
- up_weight: bfloat16 [16, 7168, 1024], P('exp', 'ctx'), may hold values from -0.0625 to 0.0625
- down_weight: bfloat16 [16, 7168, 1024], P('exp', 'ctx'), may hold values from -0.0625 to 0.0625
Outputs:
- query_grad: bfloat16 [2048, 64, 576], P('ctx', 'exp')
- latent_grad: bfloat16 [2048, 576], P('ctx')
- input_grad: bfloat16 [2048, 7168], P('exp', 'ctx')
- gate_grad: bfloat16 [16, 7168, 1024], P('exp', 'ctx')
- up_grad: bfloat16 [16, 7168, 1024], P('exp', 'ctx')
- down_grad: bfloat16 [16, 7168, 1024], P('exp', 'ctx')
Inputs may be any that keep to these rules, and one draw needn't show every extreme that they name: `expert_ids`: among the 128 rows of one index of exp no expert is named by more than 16 rows; in some such block one expert is named by exactly 16.
All inputs are finite; a program needn't handle non-finite values.
Results may differ from a plain program's by a relative error of at most 0.0053.
Values may be sent and summed in bfloat16 or wider, within the bound.
A program may use at most 128 MiB of HBM per device.

v0:
```python
import jax
import jax.numpy as jnp
from jax import lax
from jax.sharding import PartitionSpec as P

score_scale = 192.0 ** (-0.5)


def weights_of(query, grad, stats, query_pos, key_rows, key_pos, latent_width):
    scores = (
        jnp.einsum("nhc,mc->hnm", query, key_rows, preferred_element_type=jnp.float32) * score_scale
    )
    logs = jnp.transpose(stats[:, 0, :]).astype(jnp.float32)
    delta = jnp.transpose(stats[:, 1, :]).astype(jnp.float32)
    causal = key_pos[None, :] <= query_pos[:, None]
    weights = jnp.where(causal[None], jnp.exp(scores - logs[:, :, None]), 0.0)
    dweights = jnp.einsum(
        "nhl,ml->hnm", grad, key_rows[:, :latent_width], preferred_element_type=jnp.float32
    )
    dscores = weights * (dweights - delta[:, :, None])
    return (weights.astype(jnp.bfloat16), dscores.astype(jnp.bfloat16))


def expert_step(gate, upper, dhidden):
    sig = jax.nn.sigmoid(gate)
    active = gate * sig
    hidden = (active * upper).astype(jnp.bfloat16)
    gate_delta = (dhidden * upper * sig * (1.0 + gate * (1.0 - sig))).astype(jnp.bfloat16)
    up_delta = (dhidden * active).astype(jnp.bfloat16)
    return (hidden, gate_delta, up_delta)


def shards(
    queries,
    out_grad,
    attn_out,
    log_totals,
    latents,
    moe_inputs,
    moe_grad,
    expert_ids,
    gate_weight,
    up_weight,
    down_weight,
):
    length = queries.shape[0]
    latent_width = out_grad.shape[2]
    row_width = latents.shape[1]
    rotary = row_width - latent_width
    first = lax.axis_index("ctx") * length
    positions = first + jnp.arange(length, dtype=jnp.int32)
    delta = jnp.sum(out_grad.astype(jnp.float32) * attn_out.astype(jnp.float32), axis=2)
    stats = jnp.stack([jnp.transpose(log_totals), delta.astype(jnp.bfloat16)], axis=1)
    context = lax.axis_size("ctx")
    start_totals = (
        jnp.zeros(queries.shape, jnp.float32),
        jnp.zeros((length * context, row_width), jnp.float32),
    )
    piece = lax.all_gather(latents, "ctx", axis=0, tiled=True)
    count = piece.shape[0]
    piece_pos = jnp.arange(count, dtype=jnp.int32)

    def visit_rows(totals):
        weights_b, dscores_b = weights_of(
            queries, out_grad, stats, positions, piece, piece_pos, latent_width
        )
        query_total = jnp.einsum(
            "hnm,mc->nhc", dscores_b, piece, preferred_element_type=jnp.float32
        )
        key_part = (
            jnp.einsum("hnm,nhc->mc", dscores_b, queries, preferred_element_type=jnp.float32)
            * score_scale
        )
        value_part = jnp.einsum(
            "hnm,nhl->ml", weights_b, out_grad, preferred_element_type=jnp.float32
        )
        key_part = key_part + jnp.pad(value_part, ((0, 0), (0, rotary)))
        return (query_total, key_part)

    def keep_both(totals):
        return totals

    query_total, key_total = lax.cond(
        jnp.int32(0) < first + length, visit_rows, keep_both, start_totals
    )
    shares = lax.all_to_all(
        key_total.reshape(context, length, row_width),
        "ctx",
        split_axis=0,
        concat_axis=0,
        tiled=True,
    )
    key_grads = jnp.sum(shares, axis=0)
    query_grad = (query_total * score_scale).astype(jnp.bfloat16)
    latent_grad = lax.psum(key_grads, "exp").astype(jnp.bfloat16)
    local_rows = moe_inputs.shape[0]
    width = moe_inputs.shape[1]
    owned = gate_weight.shape[0]
    groups = lax.axis_size("exp")
    experts = owned * groups
    depth = max(2, 2 * local_rows // experts)
    chosen = expert_ids[:, 0]
    onehot = (chosen[:, None] == jnp.arange(experts, dtype=jnp.int32)[None, :]).astype(jnp.int32)
    earlier = jnp.cumsum(onehot, axis=0) - onehot
    slot = chosen * depth + jnp.sum(earlier * onehot, axis=1)
    empty = jnp.zeros((experts * depth, width), jnp.bfloat16)
    outgoing = empty.at[slot].set(moe_inputs).reshape(groups, owned * depth, width)
    outgoing_grad = empty.at[slot].set(moe_grad).reshape(groups, owned * depth, width)
    arrived, arrived_grad = (
        lax.all_to_all(outgoing, "exp", split_axis=0, concat_axis=0, tiled=True),
        lax.all_to_all(outgoing_grad, "exp", split_axis=0, concat_axis=0, tiled=True),
    )
    rows_in = arrived.reshape(groups, owned, depth, width)
    rows_grad = arrived_grad.reshape(groups, owned, depth, width)
    gate_part = jnp.einsum(
        "sjbd,jdf->sjbf", rows_in, gate_weight, preferred_element_type=jnp.float32
    )
    up_part = jnp.einsum("sjbd,jdf->sjbf", rows_in, up_weight, preferred_element_type=jnp.float32)
    dhidden_part = jnp.einsum(
        "sjbd,jdf->sjbf", rows_grad, down_weight, preferred_element_type=jnp.float32
    )
    gate, upper, dhidden = lax.psum((gate_part, up_part, dhidden_part), "ctx")
    hidden, gate_delta, up_delta = expert_step(gate, upper, dhidden)
    back = jnp.einsum("sjbf,jdf->sjbd", gate_delta, gate_weight, preferred_element_type=jnp.float32)
    back = back + jnp.einsum(
        "sjbf,jdf->sjbd", up_delta, up_weight, preferred_element_type=jnp.float32
    )
    back = back.astype(jnp.bfloat16).reshape(groups, owned * depth, width)
    returned = lax.all_to_all(back, "exp", split_axis=0, concat_axis=0, tiled=True).reshape(
        experts * depth, width
    )
    input_grad = returned[slot]
    gate_grad = jnp.einsum(
        "sjbd,sjbf->jdf", rows_in, gate_delta, preferred_element_type=jnp.float32
    ).astype(jnp.bfloat16)
    up_grad = jnp.einsum(
        "sjbd,sjbf->jdf", rows_in, up_delta, preferred_element_type=jnp.float32
    ).astype(jnp.bfloat16)
    down_grad = jnp.einsum(
        "sjbd,sjbf->jdf", rows_grad, hidden, preferred_element_type=jnp.float32
    ).astype(jnp.bfloat16)
    return (query_grad, latent_grad, input_grad, gate_grad, up_grad, down_grad)


def solution(mesh):
    placed = (
        P("ctx", "exp", None),
        P("ctx", "exp", None),
        P("ctx", "exp", None),
        P("exp", "ctx"),
        P("ctx", None),
        P("exp", "ctx"),
        P("exp", "ctx"),
        P("exp", None),
        P("exp", "ctx", None),
        P("exp", "ctx", None),
        P("exp", "ctx", None),
    )
    return jax.shard_map(
        shards,
        mesh=mesh,
        in_specs=placed,
        out_specs=(
            P("ctx", "exp", None),
            P("ctx", None),
            P("exp", "ctx"),
            P("exp", "ctx", None),
            P("exp", "ctx", None),
            P("exp", "ctx", None),
        ),
        check_vma=False,
    )
```

profile of v0, /device:TPU:32, one launch (start us, length us, event | category | flops | bytes accessed | tf_op | source)
XLA Modules:
  0.0 416.6 jit_solution(5210272878412359371)
XLA Ops:
  10.6 1.6 scatter_custom_fusion.1
  12.3 15.2 %all-to-all-start.2 = ((bf16[16,16,224]{2,1,0:T(8,128)(2,1)}), bf16[16,16,224]{2,1,0:T(8,128)(2,1)S(1)}, u32[]{:S(2)}, u32[]{:S(2)}) async-start(bf16[16,16,224]{2,1,0:T(8,128)(2,1)} %bitcast.19), calls=%async_computation.2 | async-start | bytes 262144 | tf_op jit(solution)/shard_map/all_to_all | solution.py:110
  28.4 1.6 scatter_custom_fusion
  30.1 11.7 %all-to-all-done.2 = bf16[16,16,224]{2,1,0:T(8,128)(2,1)S(1)} async-done(((bf16[16,16,224]{2,1,0:T(8,128)(2,1)}), bf16[16,16,224]{2,1,0:T(8,128)(2,1)S(1)}, u32[]{:S(2)}, u32[]{:S(2)}) %all-to-all-start.2) | async-done | bytes 114720 | tf_op jit(solution)/shard_map/all_to_all | solution.py:110
  41.7 4.3 %all-to-all-start.1 = ((bf16[16,16,224]{2,1,0:T(8,128)(2,1)}), bf16[16,16,224]{2,1,0:T(8,128)(2,1)S(1)}, u32[]{:S(2)}, u32[]{:S(2)}) async-start(bf16[16,16,224]{2,1,0:T(8,128)(2,1)} %bitcast.13), calls=%async_computation.1 | async-start | bytes 262144 | tf_op jit(solution)/shard_map/all_to_all | solution.py:111
  46.1 1.3 convolution_bitcast_fusion.2
  47.4 1.3 convolution_bitcast_fusion.3
  48.7 10.8 %all-to-all-done.1 = bf16[16,16,224]{2,1,0:T(8,128)(2,1)S(1)} async-done(((bf16[16,16,224]{2,1,0:T(8,128)(2,1)}), bf16[16,16,224]{2,1,0:T(8,128)(2,1)S(1)}, u32[]{:S(2)}, u32[]{:S(2)}) %all-to-all-start.1) | async-done | bytes 114720 | tf_op jit(solution)/shard_map/all_to_all | solution.py:111
  59.5 1.3 convolution_bitcast_fusion.4
  61.5 133.6 %all-reduce.5.cloned.1.call-done = (f32[16,1,16,1024]{3,2,0,1:T(8,128)}, f32[16,1,16,1024]{3,2,0,1:T(8,128)}, f32[16,1,16,1024]{3,2,0,1:T(8,128)}) async-done(((f32[16,1,16,1024]{3,2,0,1:T(8,128)}, f32[16,1,16,1024]{3,2,0,1:T(8,128)}, f32[16,1,16,1024]{3,2,0,1:T(8,128)}), (f32[16,1,16,1024]{3,2,0,1:T(8,128)}, f32[16,1,16,1024]{3,2,0,1:T(8,128)}, f32[16,1,16,1024]{3,2,0,1:T(8,128)})) %all-reduce.5.cloned.1.call-update) | async-done | bytes 3145744 | tf_op jit(solution)/shard_map/psum | solution.py:122
  195.2 2.5 fusion.29
  199.9 12.7 %all-to-all-start.3 = ((bf16[16,16,224]{2,1,0:T(8,128)(2,1)}), bf16[16,16,224]{2,1,0:T(8,128)(2,1)S(1)}, u32[]{:S(2)}, u32[]{:S(2)}) async-start(bf16[16,16,224]{2,1,0:T(8,128)(2,1)} %fusion.27), calls=%async_computation.3 | async-start | bytes 262144 | tf_op jit(solution)/shard_map/all_to_all | solution.py:129
  213.7 44.0 %all-gather.2.cloned.1.call-done = bf16[2048,576]{1,0:T(8,128)(2,1)} async-done(((bf16[64,576]{1,0:T(8,128)(2,1)}), bf16[2048,576]{1,0:T(8,128)(2,1)}) %all-gather.2.cloned.1.call-update) | async-done | bytes 2359312 | tf_op jit(solution)/shard_map/all_gather | solution.py:59
  257.8 14.2 %conditional.1 = (f32[2048,576]{0,1:T(8,128)}, f32[64,4,576]{2,1,0:T(4,128)S(1)}) conditional(s32[]{:T(128)} %convert_element_type.71, () %tuple.16, (s32[2048]{0:T(1024)S(1)}, s32[]{:T(128)}, s32[64]{0:T(128)S(1)}, bf16[2048,576]{1,0:T(8,128)(2,1)}, bf16[64,4,576]{2,1,0:T(4,128)(2,1)}, /*index=5*/bf16[4,64]{1,0:T(4,128)(2,1)S(1)}, ...), branch_computations={%region_1.0_spmd, %region_2.3_spmd} | conditional | flops 2891841792 | bytes 59914088 | solution.py:83
  258.0 2.9 fusion.6
  260.9 3.6 convolution_bitcast_fusion
  264.6 2.5 fusion.10
  267.6 3.0 fusion
  272.0 5.8 %copy.52 = f32[2048,576]{1,0:T(8,128)} copy(f32[2048,576]{0,1:T(8,128)} %get-tuple-element.35) | data formatting | bytes 9437184 | tf_op jit(solution)/shard_map/cond | solution.py:83
  277.8 5.5 %all-to-all-start = ((f32[32,64,576]{2,1,0:T(8,128)}), f32[32,64,576]{2,1,0:T(8,128)}, u32[]{:S(2)}, u32[]{:S(2)}) async-start(f32[32,64,576]{2,1,0:T(8,128)} %bitcast.125), calls=%async_computation | async-start | bytes 10485760 | tf_op jit(solution)/shard_map/all_to_all | solution.py:86
  286.1 1.3 fusion.24
  289.8 59.2 %all-to-all-done = f32[32,64,576]{2,1,0:T(8,128)} async-done(((f32[32,64,576]{2,1,0:T(8,128)}), f32[32,64,576]{2,1,0:T(8,128)}, u32[]{:S(2)}, u32[]{:S(2)}) %all-to-all-start) | async-done | bytes 4718624 | tf_op jit(solution)/shard_map/all_to_all | solution.py:86
  349.0 2.8 reduce_sum.30
  351.8 57.9 %all-reduce.6 = bf16[64,576]{1,0:T(8,128)(2,1)} all-reduce(f32[64,576]{1,0:T(8,128)S(1)} %reduce_sum.30), channel_id=1, replica_groups=mesh['ctx'=32,'exp'=16] {'exp'}, use_global_device_ids=true, to_apply=%region_4.5 | all-reduce | flops 36864 | bytes 221184 | tf_op jit(solution)/shard_map/psum | solution.py:95
  (52 shorter events, 15.8 us)
Async XLA Ops:
  7.2 38.9 %copy-start = (bf16[1,224,1024]{2,1,0:T(8,128)(2,1)S(1)}, bf16[1,224,1024]{2,1,0:T(8,128)(2,1)}, u32[]{:S(2)}) copy-start(bf16[1,224,1024]{2,1,0:T(8,128)(2,1)} %param.21) | copy-start | bytes 1376260
  7.2 40.2 %copy-start.4 = (bf16[1,224,1024]{2,1,0:T(8,128)(2,1)S(1)}, bf16[1,224,1024]{2,1,0:T(8,128)(2,1)}, u32[]{:S(2)}) copy-start(bf16[1,224,1024]{2,1,0:T(8,128)(2,1)} %param.22) | copy-start | bytes 1376260
  7.2 52.3 %copy-start.7 = (bf16[1,224,1024]{2,1,0:T(8,128)(2,1)S(1)}, bf16[1,224,1024]{2,1,0:T(8,128)(2,1)}, u32[]{:S(2)}) copy-start(bf16[1,224,1024]{2,1,0:T(8,128)(2,1)} %param.23) | copy-start | bytes 1376260
  12.3 29.4 %all-to-all-start.2 = ((bf16[16,16,224]{2,1,0:T(8,128)(2,1)}), bf16[16,16,224]{2,1,0:T(8,128)(2,1)S(1)}, u32[]{:S(2)}, u32[]{:S(2)}) async-start(bf16[16,16,224]{2,1,0:T(8,128)(2,1)} %bitcast.19), calls=%async_computation.2 | async-start | bytes 262144 | tf_op jit(solution)/shard_map/all_to_all | solution.py:110
  41.7 17.8 %all-to-all-start.1 = ((bf16[16,16,224]{2,1,0:T(8,128)(2,1)}), bf16[16,16,224]{2,1,0:T(8,128)(2,1)S(1)}, u32[]{:S(2)}, u32[]{:S(2)}) async-start(bf16[16,16,224]{2,1,0:T(8,128)(2,1)} %bitcast.13), calls=%async_computation.1 | async-start | bytes 262144 | tf_op jit(solution)/shard_map/all_to_all | solution.py:111
  46.0 149.1 %all-reduce.5.cloned.1.call-start = ((), (), s32[]{:S(2)}) async-start(), calls=%async_computation.5 | async-start | bytes 6291456 | tf_op jit(solution)/shard_map/psum | solution.py:122
  60.8 197.0 %all-gather.2.cloned.1.call-start = ((), (), s32[]{:S(2)}) async-start(), calls=%async_computation.4 | async-start | bytes 2703360 | tf_op jit(solution)/shard_map/all_gather | solution.py:59
  195.2 17.4 %copy-start.9 = (bf16[64,4,512]{2,1,0:T(4,128)(2,1)S(1)}, bf16[64,4,512]{2,1,0:T(4,128)(2,1)}, u32[]{:S(2)}) copy-start(bf16[64,4,512]{2,1,0:T(4,128)(2,1)} %param.15) | copy-start | bytes 786436
  197.7 0.8 copy-start.2
  197.7 60.0 %copy-start.10 = (bf16[4,64]{1,0:T(4,128)(2,1)S(1)}, bf16[4,64]{1,0:T(4,128)(2,1)}, u32[]{:S(2)}) copy-start(bf16[4,64]{1,0:T(4,128)(2,1)} %param.16) | copy-start | bytes 1540
  199.9 77.9 %all-to-all-start.3 = ((bf16[16,16,224]{2,1,0:T(8,128)(2,1)}), bf16[16,16,224]{2,1,0:T(8,128)(2,1)S(1)}, u32[]{:S(2)}, u32[]{:S(2)}) async-start(bf16[16,16,224]{2,1,0:T(8,128)(2,1)} %fusion.27), calls=%async_computation.3 | async-start | bytes 262144 | tf_op jit(solution)/shard_map/all_to_all | solution.py:129
  264.6 2.9 copy-start.1
  264.6 3.0 copy-start.8
  267.6 3.0 copy-start.11
  277.8 5.5 %copy-start.3 = (bf16[16,1,16,1024]{3,2,0,1:T(8,128)(2,1)S(1)}, bf16[16,1,16,1024]{3,2,0,1:T(8,128)(2,1)}, u32[]{:S(2)}) copy-start(bf16[16,1,16,1024]{3,2,0,1:T(8,128)(2,1)} %copy-done.2) | copy-start | bytes 1572868
  277.8 71.3 %all-to-all-start = ((f32[32,64,576]{2,1,0:T(8,128)}), f32[32,64,576]{2,1,0:T(8,128)}, u32[]{:S(2)}, u32[]{:S(2)}) async-start(f32[32,64,576]{2,1,0:T(8,128)} %bitcast.125), calls=%async_computation | async-start | bytes 10485760 | tf_op jit(solution)/shard_map/all_to_all | solution.py:86
  284.4 1.2 copy-start.5
  284.4 1.7 copy-start.6
Sparse Core Ops, SparseCore 0:
  60.9 134.2 all-reduce.4
  198.3 59.4 all-gather.1
where the time goes:
time: 417 us
  waiting for transfers between devices  260 us (62%)
  blocking collectives  57.9 us (14%)
  starting transfers between devices  37.8 us (9%)
  matrix products  21.7 us (5%)
  local copies, waits for them, and re-layouts  14.8 us (4%)
  between operations  14.2 us (3%)
  other arithmetic  10.1 us (2%)
    psum x1, waiting for transfers between devices, shards(): gate, upper, dhidden = lax.psum((gate_part, up_part, dhidden_part), 'ctx')  134 us
    all_to_all x1, waiting for transfers between devices, shards(): lax.all_to_all(key_total.reshape(context, length, row_width), 'ctx', spli...  59.2 us
    psum x1, blocking collectives, shards(): latent_grad = lax.psum(key_grads, 'exp').astype(jnp.bfloat16)  57.9 us
    all_gather x1, waiting for transfers between devices, shards(): piece = lax.all_gather(latents, 'ctx', axis=0, tiled=True)  44 us
    all_to_all x1, starting transfers between devices, shards(): lax.all_to_all(outgoing, 'exp', split_axis=0, concat_axis=0, tiled=True)  15.2 us
    all_to_all x1, starting transfers between devices, shards(): lax.all_to_all(back, 'exp', split_axis=0, concat_axis=0, tiled=True)  12.7 us
    all_to_all x1, waiting for transfers between devices, shards(): lax.all_to_all(outgoing, 'exp', split_axis=0, concat_axis=0, tiled=True)  11.7 us
    all_to_all x1, waiting for transfers between devices, shards(): lax.all_to_all(outgoing_grad, 'exp', split_axis=0, concat_axis=0, tiled=T...  10.8 us
  transfers between devices with their start and end apart: 6, of which 5 were waited for; matrix products, arithmetic and copies ran while one was open for 9% of the time, Pallas kernels for 0%

commit v1 on v0

v1 whole, which is shorter than its diff:
```python
import functools
import math

import jax
import jax.numpy as jnp
from jax import lax
from jax.experimental import pallas as pl
from jax.experimental.pallas import tpu as pltpu
from jax.sharding import PartitionSpec as P

MESH = pl.DeviceIdType.MESH
score_scale = 192.0 ** (-0.5)
BF = jnp.bfloat16
F32 = jnp.float32

K_LAT, K_LATF, K_TOK, K_PAIR, K_SUM, K_DEL, K_DELF, K_BACK, K_KPAIR, K_KSUM, K_ZSUM, K_ZOUT = range(12)
KINDS = 12
L_Q, L_G, L_A, L_WG, L_WU, L_WD = range(6)


def nn(a, b):
    return jnp.dot(a, b, preferred_element_type=F32)


def nt(a, b):
    return lax.dot_general(a, b, (((1,), (1,)), ((), ())), preferred_element_type=F32)


def tn(a, b):
    return lax.dot_general(a, b, (((0,), (0,)), ((), ())), preferred_element_type=F32)


def expert_step(gate, upper, dhidden):
    sig = jax.nn.sigmoid(gate)
    active = gate * sig
    hidden = (active * upper).astype(BF)
    gate_delta = (dhidden * upper * sig * (1.0 + gate * (1.0 - sig))).astype(BF)
    up_delta = (dhidden * active).astype(BF)
    return hidden, gate_delta, up_delta


def body(
    chips,
    side,
    groups,
    q_in,
    g_in,
    a_in,
    log_in,
    lat_in,
    x_in,
    xg_in,
    ids_in,
    wg_in,
    wu_in,
    wd_in,
    qg_out,
    lg_out,
    ig_out,
    gg_out,
    ug_out,
    dg_out,
    q3,
    g3,
    a3,
    wg,
    wu,
    wd,
    q_ref,
    g_ref,
    logs_row,
    delta_row,
    place,
    obuf,
    arr,
    pair_out,
    pair_in,
    own,
    sum_out,
    sum_in,
    dl,
    back_out,
    ret,
    lat_all,
    qacc,
    kp,
    kp_b,
    kpair_in,
    ksum_out,
    ksum_in,
    zpart,
    zsum_in,
    zfin,
    zout,
    send_sem,
    recv_sem,
    local_sem,
):
    c = lax.axis_index("ctx")
    z = lax.axis_index("exp")
    chip = c // 2
    core = c % 2
    sib = (chip * 2 + (1 - core), z)
    length = lat_in.shape[0]
    heads = q_in.shape[1]
    rows = length * heads
    width = x_in.shape[0]
    latent = g_in.shape[2]
    full = lat_in.shape[1]
    half = wg_in.shape[1] // 2
    blk = 16
    tokens = x_in.shape[1]
    owners = min(4, groups)
    spacing = groups // owners
    share = length // owners

    def plane(s):
        y = (chip // side + s // side) % side
        x = (chip % side + s % side) % side
        return y * side + x

    def plane_back(s):
        y = (chip // side + side - s // side) % side
        x = (chip % side + side - s % side) % side
        return y * side + x

    def to(src, dst, kind, si, ri, dev):
        return pltpu.make_async_remote_copy(
            src_ref=src,
            dst_ref=dst,
            send_sem=send_sem.at[kind, si],
            recv_sem=recv_sem.at[kind, ri],
            device_id=dev,
            device_id_type=MESH,
        )

    def arrived(dst, kind, ri):
        to(dst, dst, kind, 0, ri, sib).wait_recv()

    def sent(src, kind, si):
        to(src, src, kind, si, 0, sib).wait_send()

    def each(lo, hi, f):
        def step(i, carry):
            f(i)
            return carry

        lax.fori_loop(lo, hi, step, 0)

    def peer(q):
        return (2 * q + core, z)

    def fetch(src, dst, i):
        return pltpu.make_async_copy(src, dst, local_sem.at[i])

    loads = [
        fetch(wg_in, wg, L_WG),
        fetch(wu_in, wu, L_WU),
        fetch(wd_in, wd, L_WD),
        fetch(q_in, q3, L_Q),
        fetch(g_in, g3, L_G),
        fetch(a_in, a3, L_A),
    ]
    for load in loads:
        load.start()

    chunk = min(256, lat_all.shape[0])
    per = chunk // length
    last = c // per
    lat_all[pl.ds(pl.multiple_of(last * chunk, chunk), chunk), :] = jnp.zeros((chunk, full), BF)
    my_rows = pl.ds(pl.multiple_of(c * length, length), length)
    lat_all[my_rows, :] = lat_in[...]

    barrier = pltpu.get_barrier_semaphore()

    def greet_plane(s):
        pl.semaphore_signal(barrier, inc=1, device_id=peer(plane(s)), device_id_type=MESH)

    def greet_line(s):
        pl.semaphore_signal(barrier, inc=1, device_id=(c, (z + s) % groups), device_id_type=MESH)

    each(1, groups, greet_line)
    each(1, chips, greet_plane)
    pl.semaphore_signal(barrier, inc=1, device_id=sib, device_id_type=MESH)

    chosen = ids_in[...]
    experts = groups
    onehot = (lax.broadcasted_iota(jnp.int32, (experts, tokens), 0) == chosen).astype(F32)
    before = lax.broadcasted_iota(jnp.int32, (tokens, tokens), 0) < lax.broadcasted_iota(
        jnp.int32, (tokens, tokens), 1
    )
    earlier = nn(onehot.astype(BF), before.astype(F32).astype(BF))
    rank = jnp.sum(earlier * onehot, axis=0, keepdims=True)
    slot = chosen * blk + rank.astype(jnp.int32)
    place[...] = (
        (lax.broadcasted_iota(jnp.int32, (experts * blk, tokens), 0) == slot)
        .astype(F32)
        .astype(BF)
    )
    obuf[0] = nt(place[...], x_in[...]).astype(BF)
    obuf[1] = nt(place[...], xg_in[...]).astype(BF)
    mine = pl.ds(pl.multiple_of(z * blk, blk), blk)
    arr[:, mine, :] = obuf[:, mine, :]

    pl.semaphore_wait(barrier, groups + chips - 1)

    def line_rows(zz):
        return pl.ds(pl.multiple_of(zz * blk, blk), blk)

    def send_tokens(s):
        zz = (z + s) % groups
        to(obuf.at[:, line_rows(zz), :], arr.at[:, mine, :], K_TOK, s, z, (c, zz)).start()

    each(1, groups, send_tokens)

    def send_latents(q):
        to(lat_all.at[my_rows, :], lat_all.at[my_rows, :], K_LAT, q, chip, peer(q)).start()

    each(chip + 1, chips, send_latents)

    @pl.when(core == 0)
    def _():
        to(lat_all.at[my_rows, :], lat_all.at[my_rows, :], K_LATF, chip, chip, sib).start()

    for i in (L_Q, L_G, L_A):
        loads[{L_Q: 3, L_G: 4, L_A: 5}[i]].wait()
    q_ref[...] = q3[...].reshape(rows, full)
    g_ref[...] = g3[...].reshape(rows, latent)
    delta = jnp.sum(
        g_ref[...].astype(F32) * a3[...].reshape(rows, latent).astype(F32), axis=1, keepdims=True
    )
    delta = delta.astype(BF).astype(F32)
    diagonal = lax.broadcasted_iota(jnp.int32, (rows, rows), 0) == lax.broadcasted_iota(
        jnp.int32, (rows, rows), 1
    )
    delta_row[...] = jnp.sum(jnp.where(diagonal, delta, 0.0), axis=0, keepdims=True)
    spread = lax.broadcasted_iota(jnp.int32, (length, rows), 0) == (
        lax.broadcasted_iota(jnp.int32, (length, rows), 1) // heads
    )
    by_head = nn(log_in[...], spread.astype(F32).astype(BF))
    of_head = lax.broadcasted_iota(jnp.int32, (heads, rows), 0) == (
        lax.broadcasted_iota(jnp.int32, (heads, rows), 1) % heads
    )
    logs_row[...] = jnp.sum(jnp.where(of_head, by_head, 0.0), axis=0, keepdims=True)

    for i in range(3):
        loads[i].wait()

    def tokens_here(s):
        zz = (z + groups - s) % groups
        arrived(arr.at[:, line_rows(zz), :], K_TOK, zz)

    each(1, groups, tokens_here)

    other_cols = pl.ds(pl.multiple_of((1 - core) * half, half), half)
    my_cols = pl.ds(pl.multiple_of(core * half, half), half)
    for j, (w, side_of) in enumerate(((wg, 0), (wu, 0), (wd, 1))):
        pair_out[j] = nn(arr[side_of], w[:, other_cols])
        to(pair_out.at[j], pair_in.at[j], K_PAIR, j, j, sib).start()
    for j, (w, side_of) in enumerate(((wg, 0), (wu, 0), (wd, 1))):
        own[j] = nn(arr[side_of], w[:, my_cols])

    def block_rows(b):
        return pl.ds(pl.multiple_of(b * length, length), length)

    def pass_latents(q):
        here = lat_all.at[block_rows(2 * q + core), :]
        arrived(here, K_LAT, q)
        to(here, here, K_LATF, q, q, sib).start()

    each(0, chip, pass_latents)

    for j in range(3):
        arrived(pair_in.at[j], K_PAIR, j)
        both = own[j] + pair_in[j]
        sum_out[:, j] = both.reshape(chips, blk, half).astype(BF)

    def send_sums(s):
        q = plane(s)
        to(sum_out.at[q], sum_in.at[chip], K_SUM, s, chip, peer(q)).start()

    each(1, chips, send_sums)
    sum_in[chip] = sum_out[chip]

    def latents_here(q):
        arrived(lat_all.at[block_rows(2 * q + 1 - core), :], K_LATF, q)

    each(0, chip + core, latents_here)
    qacc[...] = jnp.zeros_like(qacc)

    def visit(m, carry):
        at = pl.ds(pl.multiple_of(m * chunk, chunk), chunk)
        keys = lat_all[at, :]
        queries = q_ref[...]
        grads = g_ref[...]
        scores = nt(keys, queries) * score_scale
        key_pos = m * chunk + lax.broadcasted_iota(jnp.int32, (chunk, rows), 0)
        query_pos = c * length + lax.broadcasted_iota(jnp.int32, (chunk, rows), 1) // heads
        weights = jnp.where(key_pos <= query_pos, jnp.exp(scores - logs_row[...]), 0.0)
        dweights = nt(keys[:, :latent], grads)
        dscores = (weights * (dweights - delta_row[...])).astype(BF)
        weights = weights.astype(BF)
        key_part = nn(dscores, queries) * score_scale
        value_part = nn(weights, grads)
        kp[at, :latent] = key_part[:, :latent] + value_part
        kp[at, latent:] = key_part[:, latent:]
        kp_b[at, :] = kp[at, :].astype(BF)
        qacc[...] += tn(dscores, keys)
        for i in range(per // 2):
            q = m * (per // 2) + i

            @pl.when(q < chip + core)
            def _():
                theirs = block_rows(2 * q + 1 - core)
                to(kp_b.at[theirs, :], kpair_in.at[q], K_KPAIR, q, q, sib).start()

        return carry

    lax.fori_loop(0, last + 1, visit, 0)
    qg_out[...] = (qacc[...] * score_scale).astype(BF)

    def sums_here(s):
        q = plane_back(s)
        arrived(sum_in.at[q], K_SUM, q)

    each(1, chips, sums_here)

    def total_of(j):
        total = sum_in[0, j].astype(F32)
        for q in range(1, chips):
            total = total + sum_in[q, j].astype(F32)
        return total

    hidden, gate_delta, up_delta = expert_step(total_of(0), total_of(1), total_of(2))
    dl[core, chip, 0] = hidden
    dl[core, chip, 1] = gate_delta
    dl[core, chip, 2] = up_delta

    def send_deltas(s):
        here = dl.at[core, chip]
        to(here, here, K_DEL, s, chip, peer(plane(s))).start()

    each(1, chips, send_deltas)
    to(dl.at[core, chip], dl.at[core, chip], K_DELF, chip, chip, sib).start()

    def add_pair(q):
        arrived(kpair_in.at[q], K_KPAIR, q)
        both = kp[block_rows(2 * q + core), :] + kpair_in[q].astype(F32)
        ksum_out[q] = both.astype(BF)
        to(ksum_out.at[q], ksum_in.at[chip], K_KSUM, q, chip, peer(q)).start()

    each(0, chip, add_pair)

    @pl.when(core == 0)
    def _():
        arrived(kpair_in.at[chip], K_KPAIR, chip)
        zpart[...] = kp[my_rows, :] + kpair_in[chip].astype(F32)

    @pl.when(core == 1)
    def _():
        zpart[...] = kp[my_rows, :]

    def pass_deltas(s):
        q = plane_back(s)
        here = dl.at[core, q]
        arrived(here, K_DEL, q)
        to(here, here, K_DELF, q, q, sib).start()

    each(1, chips, pass_deltas)

    def deltas_here(q):
        arrived(dl.at[1 - core, q], K_DELF, q)

    each(0, chips, deltas_here)

    def delta_of(h, j):
        return dl[h, :, j].reshape(chips * blk, half)

    back = jnp.zeros((groups * blk, width), F32)
    for h in range(2):
        cols = slice(h * half, (h + 1) * half)
        back = back + nt(delta_of(h, 1), wg[:, cols]) + nt(delta_of(h, 2), wu[:, cols])
    back_out[...] = back.astype(BF)

    def send_back(s):
        zz = (z + s) % groups
        to(back_out.at[line_rows(zz), :], ret.at[mine, :], K_BACK, s, z, (c, zz)).start()

    each(1, groups, send_back)
    ret[mine, :] = back_out[mine, :]

    def add_sum(q):
        arrived(ksum_in.at[q], K_KSUM, q)
        zpart[...] += ksum_in[q].astype(F32)

    each(chip + 1, chips, add_sum)
    zfin[...] = zpart[...].astype(BF)

    def share_rows(i):
        return pl.ds(pl.multiple_of(i * share, share), share)

    def owner_z(i):
        return i * spacing + (spacing // 2) * core

    def send_share(i):
        @pl.when(owner_z(i) != z)
        def _():
            to(
                zfin.at[share_rows(i), :], zsum_in.at[z], K_ZSUM, i, z, (c, owner_z(i))
            ).start()

    each(0, owners, send_share)

    for h in range(2):
        cols = slice(h * half, (h + 1) * half)
        gg_out[:, cols] = tn(arr[0], delta_of(h, 1)).astype(BF)
        ug_out[:, cols] = tn(arr[0], delta_of(h, 2)).astype(BF)
        dg_out[:, cols] = tn(arr[1], delta_of(h, 0)).astype(BF)

    mine_share = z // spacing
    is_owner = owner_z(mine_share) == z

    @pl.when(is_owner)
    def _():
        def shares_here(s):
            zz = (z + s) % groups
            arrived(zsum_in.at[zz], K_ZSUM, zz)

        each(1, groups, shares_here)
        zsum_in[z] = zfin[share_rows(mine_share), :]
        total = zsum_in[0].astype(F32)
        for zz in range(1, groups):
            total = total + zsum_in[zz].astype(F32)
        zout[share_rows(mine_share), :] = total.astype(BF)

        def send_rows(s):
            zz = (z + s) % groups
            there = zout.at[share_rows(mine_share), :]
            to(there, there, K_ZOUT, s, mine_share, (c, zz)).start()

        each(1, groups, send_rows)

    def back_here(s):
        zz = (z + groups - s) % groups
        arrived(ret.at[line_rows(zz), :], K_BACK, zz)

    each(1, groups, back_here)
    ig_out[...] = tn(ret[...], place[...]).astype(BF)

    def rows_here(i):
        @pl.when(owner_z(i) != z)
        def _():
            arrived(zout.at[share_rows(i), :], K_ZOUT, i)

    each(0, owners, rows_here)
    lg_out[...] = zout[...]

    one_block = lat_all.at[my_rows, :]
    each(chip + 1, chips, lambda q: sent(one_block, K_LAT, q))
    each(0, chip, lambda q: sent(one_block, K_LATF, q))

    @pl.when(core == 0)
    def _():
        sent(one_block, K_LATF, chip)

    each(1, groups, lambda s: sent(obuf.at[:, mine, :], K_TOK, s))
    for j in range(3):
        sent(pair_out.at[j], K_PAIR, j)
    each(1, chips, lambda s: sent(sum_out.at[0], K_SUM, s))
    each(1, chips, lambda s: sent(dl.at[0, 0], K_DEL, s))
    each(0, chips, lambda q: sent(dl.at[0, 0], K_DELF, q))
    each(0, chip + core, lambda q: sent(ksum_out.at[0], K_KPAIR, q))
    each(0, chip, lambda q: sent(ksum_out.at[0], K_KSUM, q))
    each(1, groups, lambda s: sent(back_out.at[mine, :], K_BACK, s))

    def share_sent(i):
        @pl.when(owner_z(i) != z)
        def _():
            sent(zfin.at[share_rows(0), :], K_ZSUM, i)

    each(0, owners, share_sent)

    @pl.when(is_owner)
    def _():
        each(1, groups, lambda s: sent(zfin.at[share_rows(0), :], K_ZOUT, s))


def shards(
    chips,
    groups,
    queries,
    out_grad,
    attn_out,
    log_totals,
    latents,
    moe_inputs,
    moe_grad,
    expert_ids,
    gate_weight,
    up_weight,
    down_weight,
):
    length, heads, full = queries.shape
    latent = out_grad.shape[2]
    rows = length * heads
    tokens, width = moe_inputs.shape
    hidden = gate_weight.shape[2]
    half = hidden // 2
    blk = 16
    slots = groups * blk
    keys = length * chips * 2
    side = math.isqrt(chips)
    vmem = pl.BlockSpec(memory_space=pltpu.VMEM)
    hbm = pl.BlockSpec(memory_space=pl.ANY)
    lanes = max(chips, groups)
    owners = min(4, groups)
    weight = (width, hidden)
    qg, lg, ig, gg, ug, dg = pl.pallas_call(
        functools.partial(body, chips, side, groups),
        out_shape=(
            jax.ShapeDtypeStruct((rows, full), BF),
            jax.ShapeDtypeStruct((length, full), BF),
            jax.ShapeDtypeStruct((width, tokens), BF),
            jax.ShapeDtypeStruct(weight, BF),
            jax.ShapeDtypeStruct(weight, BF),
            jax.ShapeDtypeStruct(weight, BF),
        ),
        in_specs=[hbm, hbm, hbm, vmem, vmem, vmem, vmem, vmem, hbm, hbm, hbm],
        out_specs=(vmem,) * 6,
        scratch_shapes=[
            pltpu.VMEM((length, heads, full), BF),
            pltpu.VMEM((length, heads, latent), BF),
            pltpu.VMEM((length, heads, latent), BF),
            pltpu.VMEM(weight, BF),
            pltpu.VMEM(weight, BF),
            pltpu.VMEM(weight, BF),
            pltpu.VMEM((rows, full), BF),
            pltpu.VMEM((rows, latent), BF),
            pltpu.VMEM((1, rows), F32),
            pltpu.VMEM((1, rows), F32),
            pltpu.VMEM((slots, tokens), BF),
            pltpu.VMEM((2, slots, width), BF),
            pltpu.VMEM((2, slots, width), BF),
            pltpu.VMEM((3, slots, half), F32),
            pltpu.VMEM((3, slots, half), F32),
            pltpu.VMEM((3, slots, half), F32),
            pltpu.VMEM((chips, 3, blk, half), BF),
            pltpu.VMEM((chips, 3, blk, half), BF),
            pltpu.VMEM((2, chips, 3, blk, half), BF),
            pltpu.VMEM((slots, width), BF),
            pltpu.VMEM((slots, width), BF),
            pltpu.VMEM((keys, full), BF),
            pltpu.VMEM((rows, full), F32),
            pltpu.VMEM((keys, full), F32),
            pltpu.VMEM((keys, full), BF),
            pltpu.VMEM((chips, length, full), BF),
            pltpu.VMEM((chips, length, full), BF),
            pltpu.VMEM((chips, length, full), BF),
            pltpu.VMEM((length, full), F32),
            pltpu.VMEM((groups, length // owners, full), BF),
            pltpu.VMEM((length, full), BF),
            pltpu.VMEM((length, full), BF),
            pltpu.SemaphoreType.DMA((KINDS, lanes)),
            pltpu.SemaphoreType.DMA((KINDS, lanes)),
            pltpu.SemaphoreType.DMA((6,)),
        ],
        compiler_params=pltpu.CompilerParams(
            collective_id=0, has_side_effects=True, vmem_limit_bytes=52 * 1024 * 1024
        ),
    )(
        queries,
        out_grad,
        attn_out,
        log_totals,
        latents,
        jnp.transpose(moe_inputs),
        jnp.transpose(moe_grad),
        expert_ids.reshape(1, tokens),
        gate_weight.reshape(weight),
        up_weight.reshape(weight),
        down_weight.reshape(weight),
    )
    return (
        qg.reshape(length, heads, full),
        lg,
        jnp.transpose(ig),
        gg.reshape((1,) + weight),
        ug.reshape((1,) + weight),
        dg.reshape((1,) + weight),
    )


def solution(mesh):
    chips = mesh.shape["ctx"] // 2
    groups = mesh.shape["exp"]
    return jax.shard_map(
        functools.partial(shards, chips, groups),
        mesh=mesh,
        in_specs=(
            P("ctx", "exp", None),
            P("ctx", "exp", None),
            P("ctx", "exp", None),
            P("exp", "ctx"),
            P("ctx", None),
            P("exp", "ctx"),
            P("exp", "ctx"),
            P("exp", None),
            P("exp", "ctx", None),
            P("exp", "ctx", None),
            P("exp", "ctx", None),
        ),
        out_specs=(
            P("ctx", "exp", None),
            P("ctx", None),
            P("exp", "ctx"),
            P("exp", "ctx", None),
            P("exp", "ctx", None),
            P("exp", "ctx", None),
        ),
        check_vma=False,
    )
```

time: 417 us -> 114 us (0.27)
  the two profiles are of different devices: /device:TPU:32 before, /device:TPU:4 now
where the time goes in v1:
time: 114 us; the launch traced here: 113 us
  Pallas kernels  101 us (89%)
  local copies, waits for them, and re-layouts  11.3 us (10%)
    pallas_call x1, Pallas kernels, shards(): pl.pallas_call(functools.partial(body, chips, side, groups), out_shape=(j...  101 us
    unnamed x25, local copies, waits for them, and re-layouts  10.4 us

profile of v1, /device:TPU:4, one launch (start us, length us, event | category | flops | bytes accessed | tf_op | source)
XLA Modules:
  0.0 113.2 jit_solution(16802702926087196066)
XLA Ops:
  0.6 0.0 copy-start.6
  0.6 0.0 copy-start.7
  0.7 0.7 copy-done.6
  1.3 0.0 copy-done.7
  1.3 1.0 copy-done
  2.3 0.0 copy-start.1
  2.3 0.9 copy-done.1
  3.2 0.0 copy-start.2
  3.2 0.9 copy-done.2
  4.2 0.0 copy-start.3
  4.2 0.9 copy-done.3
  5.1 0.0 copy-start.4
  5.1 0.8 copy-done.4
  5.9 0.0 copy-start.5
  5.9 0.8 copy-done.5
  6.7 101.3 %shard_map.154 = (bf16[256,576]{1,0:T(8,128)(2,1)S(1)}, bf16[64,576]{1,0:T(8,128)(2,1)S(1)}, bf16[224,128]{1,0:T(8,128)(2,1)S(1)}, bf16[224,1024]{1,0:T(8,128)(2...) custom-call(bf16[64,4,576]{2,1,0:T(4,128)(2,1)S(1)} %copy-done, bf16[64,4,512]{2,1,0:T(4,128)(2,1)S(1)} %copy-done.1, ...), custom_call_target="tpu_custom_call" | custom-call | tf_op jit(solution)/shard_map/pallas_call | solution.py:518
  108.0 0.8 reshape.40
  108.8 0.6 copy.22
  109.4 0.6 copy.23
  110.1 0.8 copy.24
  110.8 0.4 copy-done.9
  111.2 0.8 copy.25
  112.0 0.4 copy-done.8
  112.4 0.8 copy.26
  (3 shorter events, 0.0 us)
Async XLA Ops:
  0.6 0.7 copy-start.6
  0.6 0.7 copy-start.7
  1.3 1.0 copy-start
  2.3 0.9 copy-start.1
  3.2 0.9 copy-start.2
  4.2 0.9 copy-start.3
  5.1 0.8 copy-start.4
  5.9 0.8 copy-start.5
  110.1 1.2 %copy-start.9 = (bf16[224,1024]{1,0:T(8,128)(2,1)S(1)}, bf16[224,1024]{1,0:T(8,128)(2,1)}, u32[]{:S(2)}) copy-start(bf16[224,1024]{1,0:T(8,128)(2,1)} %get-tuple-element.16) | copy-start | bytes 1376260
  111.2 1.2 %copy-start.8 = (bf16[224,1024]{1,0:T(8,128)(2,1)S(1)}, bf16[224,1024]{1,0:T(8,128)(2,1)}, u32[]{:S(2)}) copy-start(bf16[224,1024]{1,0:T(8,128)(2,1)} %get-tuple-element.17) | copy-start | bytes 1376260

commit v2 on v1

v2 whole, which is shorter than its diff:
```python
import functools
import math

import jax
import jax.numpy as jnp
from jax import lax
from jax.experimental import pallas as pl
from jax.experimental.pallas import tpu as pltpu
from jax.sharding import PartitionSpec as P

MESH = pl.DeviceIdType.MESH
VMEM = 63 * 1024 * 1024
score_scale = 192.0 ** (-0.5)
BF = jnp.bfloat16
F32 = jnp.float32

(
    K_LAT,
    K_LATF,
    K_TOK,
    K_TOKG,
    K_PAIR,
    K_SUM,
    K_SUMD,
    K_DEL,
    K_DELF,
    K_BACK,
    K_KPAIR,
    K_KSUM,
    K_KCOL,
    K_ZSUM,
    K_ZOUT,
) = range(15)
KINDS = 15
(
    L_LAT,
    L_IDS,
    L_X,
    L_XG,
    L_WG,
    L_WU,
    L_WD,
    L_Q,
    L_G,
    L_A,
    L_LOG,
    O_QG,
    O_LG,
    O_IG,
    O_GG,
    O_UG,
    O_DG,
) = range(17)


def nn(a, b):
    return jnp.dot(a, b, preferred_element_type=F32)


def nt(a, b):
    return lax.dot_general(a, b, (((1,), (1,)), ((), ())), preferred_element_type=F32)


def tn(a, b):
    return lax.dot_general(a, b, (((0,), (0,)), ((), ())), preferred_element_type=F32)


def expert_step(gate, upper, dhidden):
    sig = jax.nn.sigmoid(gate)
    active = gate * sig
    hidden = (active * upper).astype(BF)
    gate_delta = (dhidden * upper * sig * (1.0 + gate * (1.0 - sig))).astype(BF)
    up_delta = (dhidden * active).astype(BF)
    return hidden, gate_delta, up_delta


def body(
    chips,
    side,
    groups,
    q_in,
    g_in,
    a_in,
    log_in,
    lat_in,
    x_in,
    xg_in,
    ids_in,
    wg_in,
    wu_in,
    wd_in,
    qg_out,
    lg_out,
    ig_out,
    gg_out,
    ug_out,
    dg_out,
    q3,
    g3,
    a3,
    logs,
    ids,
    xt,
    xgt,
    wg,
    wu,
    wd,
    q_ref,
    g_ref,
    logs_row,
    delta_row,
    place,
    obuf,
    arr,
    pair_out,
    pair_in,
    own,
    sum_out,
    sum_in,
    dl,
    back_out,
    ret,
    lat_all,
    qacc,
    kp,
    kp_b,
    kpair_in,
    ksum_out,
    ksum_in,
    kcol_out,
    kcol_in,
    zpart,
    zsum_in,
    zfin,
    zout,
    igt,
    lgt,
    lat_own,
    gg,
    ug,
    dg,
    send_sem,
    recv_sem,
    local_sem,
):
    c = lax.axis_index("ctx")
    z = lax.axis_index("exp")
    chip = lax.div(c, 2)
    core = lax.rem(c, 2)
    sib = (chip * 2 + (1 - core), z)
    length, full = lat_in.shape
    heads = q_in.shape[1]
    rows = length * heads
    width, tokens = x_in.shape
    latent = g_in.shape[2]
    half = wg_in.shape[1] // 2
    blk = 16
    experts = groups
    owners = min(4, groups)
    spacing = groups // owners
    share = length // owners
    chunk = min(256, lat_all.shape[0])
    per = chunk // length
    last = lax.div(c, per)
    here_y = lax.div(chip, side)
    here_x = lax.rem(chip, side)

    def plane(s):
        y = lax.rem(here_y + lax.div(s, side), side)
        x = lax.rem(here_x + lax.rem(s, side), side)
        return y * side + x

    def plane_back(s):
        y = lax.rem(here_y + side - lax.div(s, side), side)
        x = lax.rem(here_x + side - lax.rem(s, side), side)
        return y * side + x

    first = here_x * (1 - core) + here_y * core
    second = here_y * (1 - core) + here_x * core

    def at(f, g):
        return (g * side + f) * (1 - core) + (f * side + g) * core

    def turned(v, s):
        return lax.rem(v + s, side)

    def ahead(s):
        return lax.rem(z + s, groups)

    def behind(s):
        return lax.rem(z + groups - s, groups)

    def to(src, dst, kind, si, ri, dev):
        return pltpu.make_async_remote_copy(
            src_ref=src,
            dst_ref=dst,
            send_sem=send_sem.at[kind, si],
            recv_sem=recv_sem.at[kind, ri],
            device_id=dev,
            device_id_type=MESH,
        )

    def arrived(dst, kind, ri):
        to(dst, dst, kind, 0, ri, sib).wait_recv()

    def sent(src, kind, si):
        to(src, src, kind, si, 0, sib).wait_send()

    def each(lo, hi, f):
        def step(i, carry):
            f(i)
            return carry

        lax.fori_loop(lo, hi, step, 0)

    def peer(q):
        return (2 * q + core, z)

    def line_rows(zz):
        return pl.ds(pl.multiple_of(zz * blk, blk), blk)

    def block_rows(b):
        return pl.ds(pl.multiple_of(b * length, length), length)

    def share_rows(i):
        return pl.ds(pl.multiple_of(i * share, share), share)

    def owner_z(i):
        return i * spacing + (spacing // 2) * core

    mine = line_rows(z)
    my_rows = block_rows(c)
    my_block = lat_all.at[my_rows, :]
    mine_share = lax.div(z, spacing)
    is_owner = owner_z(mine_share) == z
    other_cols = pl.ds(pl.multiple_of((1 - core) * half, half), half)
    my_cols = pl.ds(pl.multiple_of(core * half, half), half)
    barrier = pltpu.get_barrier_semaphore()

    def gather_start(block, kind):
        for s in range(1, side):
            to(block(chip), block(chip), kind, s, chip, peer(at(turned(first, s), second))).start()

    def gather_second(block, kind, f):
        held = at(f, second)
        for s in range(1, side):
            si = side * (1 + lax.rem(f - first + side, side)) + s
            to(block(held), block(held), kind, si, held, peer(at(first, turned(second, s)))).start()

    def gather_first_rest(block, kind, fkind):
        def step(s):
            q = at(turned(first, side - s), second)
            arrived(block(q), kind, q)
            gather_second(block, kind, turned(first, side - s))
            to(block(q), block(q), fkind, q, q, sib).start()

        each(1, side, step)

    def gather_second_rest(block, kind, fkind):
        def step(i):
            f = turned(first, side - lax.rem(i, side))
            q = at(f, turned(second, side - lax.div(i, side)))
            arrived(block(q), kind, q)
            to(block(q), block(q), fkind, q, q, sib).start()

        each(side, chips, step)

    def gather_pending(block, kind, fkind):
        pending.append(lambda: each(1, side, lambda s: sent(block, kind, s)))
        pending.append(
            lambda: each(
                0,
                side * (side - 1),
                lambda i: sent(
                    block, kind, side * (1 + lax.div(i, side - 1)) + 1 + lax.rem(i, side - 1)
                ),
            )
        )
        pending.append(lambda: each(0, chips, lambda q: sent(block, fkind, q)))

    def lat_block(q):
        return lat_all.at[block_rows(2 * q + core), :]

    def delta_block(q):
        return dl.at[core, q]

    copies = {}

    def start(src, dst, i):
        copies[i] = pltpu.make_async_copy(src, dst, local_sem.at[i])
        copies[i].start()

    def ready(*which):
        for i in which:
            copies.pop(i).wait()

    pending = []

    def load():
        ksum_out[...] = jnp.zeros_like(ksum_out)
        start(ids_in, ids, L_IDS)
        start(x_in, xt, L_X)
        start(xg_in, xgt, L_XG)
        start(lat_in, lat_own, L_LAT)
        start(wg_in, wg, L_WG)
        start(wu_in, wu, L_WU)
        start(wd_in, wd, L_WD)
        start(q_in, q3, L_Q)
        start(g_in, g3, L_G)
        start(a_in, a3, L_A)
        start(log_in, logs, L_LOG)

    def greet():
        def greet_line(s):
            pl.semaphore_signal(
                barrier, inc=1, device_id=(c, ahead(s)), device_id_type=MESH
            )

        def greet_plane(s):
            pl.semaphore_signal(barrier, inc=1, device_id=peer(plane(s)), device_id_type=MESH)

        each(1, groups, greet_line)
        each(1, chips, greet_plane)
        pl.semaphore_signal(barrier, inc=1, device_id=sib, device_id_type=MESH)

    def dispatch():
        ready(L_IDS, L_X, L_XG)
        chosen = ids[...]
        onehot = (lax.broadcasted_iota(jnp.int32, (experts, tokens), 0) == chosen).astype(F32)
        before = lax.broadcasted_iota(jnp.int32, (tokens, tokens), 0) < lax.broadcasted_iota(
            jnp.int32, (tokens, tokens), 1
        )
        earlier = nn(onehot.astype(BF), before.astype(F32).astype(BF))
        rank = jnp.sum(earlier * onehot, axis=0, keepdims=True)
        slot = chosen * blk + rank.astype(jnp.int32)
        place[...] = (
            (lax.broadcasted_iota(jnp.int32, (experts * blk, tokens), 0) == slot)
            .astype(F32)
            .astype(BF)
        )
        obuf[0, :, :width] = nt(place[...], xt[...]).astype(BF)
        obuf[1, :, :width] = nt(place[...], xgt[...]).astype(BF)
        arr[:, mine, :] = obuf[:, mine, :]

    def met():
        pl.semaphore_wait(barrier, groups + chips - 1)

    def send_tokens_of(part, kind):
        def step(s):
            zz = ahead(s)
            to(obuf.at[part, line_rows(zz), :], arr.at[part, mine, :], kind, s, z, (c, zz)).start()

        each(1, groups, step)
        pending.append(lambda: each(1, groups, lambda s: sent(obuf.at[0, mine, :], kind, s)))

    def send_inputs():
        send_tokens_of(0, K_TOK)

    def send_grads():
        send_tokens_of(1, K_TOKG)

    def send_latents():
        ready(L_LAT)
        lat_all[my_rows, :full] = lat_own[...]
        gather_start(lat_block, K_LAT)
        gather_second(lat_block, K_LAT, first)
        to(my_block, my_block, K_LATF, chip, chip, sib).start()
        gather_pending(my_block, K_LAT, K_LATF)

    def pass_latents():
        gather_first_rest(lat_block, K_LAT, K_LATF)

    def pass_latents_on():
        gather_second_rest(lat_block, K_LAT, K_LATF)

    def row_values():
        ready(L_Q, L_G, L_A, L_LOG)
        q_ref[...] = q3[...].reshape(rows, full)
        g_ref[...] = g3[...].reshape(rows, latent)
        delta = jnp.sum(
            g_ref[...].astype(F32) * a3[...].reshape(rows, latent).astype(F32),
            axis=1,
            keepdims=True,
        )
        delta = delta.astype(BF).astype(F32)
        diagonal = lax.broadcasted_iota(jnp.int32, (rows, rows), 0) == lax.broadcasted_iota(
            jnp.int32, (rows, rows), 1
        )
        delta_row[...] = jnp.sum(jnp.where(diagonal, delta, 0.0), axis=0, keepdims=True)
        spread = lax.broadcasted_iota(jnp.int32, (length, rows), 0) == (
            lax.broadcasted_iota(jnp.int32, (length, rows), 1) // heads
        )
        by_head = nn(logs[...], spread.astype(F32).astype(BF))
        of_head = lax.broadcasted_iota(jnp.int32, (heads, rows), 0) == (
            lax.broadcasted_iota(jnp.int32, (heads, rows), 1) % heads
        )
        logs_row[...] = jnp.sum(jnp.where(of_head, by_head, 0.0), axis=0, keepdims=True)

    def tokens_here_of(part, kind):
        def step(s):
            zz = behind(s)
            arrived(arr.at[part, line_rows(zz), :], kind, zz)

        each(1, groups, step)

    def project_of(j, w, part):
        pair_out[j] = nn(arr[part, :, :width], w[:, other_cols])
        to(pair_out.at[j], pair_in.at[j], K_PAIR, j, j, sib).start()
        pending.append(lambda: sent(pair_out.at[j], K_PAIR, j))

    def project_inputs():
        tokens_here_of(0, K_TOK)
        ready(L_WG, L_WU)
        project_of(0, wg, 0)
        project_of(1, wu, 0)
        own[0] = nn(arr[0, :, :width], wg[:, my_cols])
        own[1] = nn(arr[0, :, :width], wu[:, my_cols])

    def project_grads():
        tokens_here_of(1, K_TOKG)
        ready(L_WD)
        project_of(2, wd, 1)
        own[2] = nn(arr[1, :, :width], wd[:, my_cols])

    def add_pair(j):
        arrived(pair_in.at[j], K_PAIR, j)
        both = own[j] + pair_in[j]
        sum_out[:, j] = both.reshape(chips, blk, half).astype(BF)
        sum_in[chip, j] = sum_out[chip, j]

    def send_sums_of(parts, kind):
        def step(s):
            q = plane(s)
            to(sum_out.at[q, parts], sum_in.at[chip, parts], kind, s, chip, peer(q)).start()

        each(1, chips, step)
        pending.append(lambda: each(1, chips, lambda s: sent(sum_out.at[0, parts], kind, s)))

    def sums_here_of(parts, kind):
        def step(s):
            q = plane_back(s)
            arrived(sum_in.at[q, parts], kind, q)

        each(1, chips, step)

    def send_input_sums():
        add_pair(0)
        add_pair(1)
        send_sums_of(pl.ds(0, 2), K_SUM)

    def send_grad_sums():
        add_pair(2)
        send_sums_of(pl.ds(2, 1), K_SUMD)

    def latents_here():
        each(0, chips, lambda q: arrived(lat_all.at[block_rows(2 * q + 1 - core), :], K_LATF, q))

    def attention():
        qacc[...] = jnp.zeros_like(qacc)

        def visit(m, carry):
            at = pl.ds(pl.multiple_of(m * chunk, chunk), chunk)
            keys = lat_all[at, :full]
            queries = q_ref[...]
            grads = g_ref[...]
            scores = nt(keys, queries) * score_scale
            key_pos = m * chunk + lax.broadcasted_iota(jnp.int32, (chunk, rows), 0)
            query_pos = c * length + lax.broadcasted_iota(jnp.int32, (chunk, rows), 1) // heads
            weights = jnp.where(key_pos <= query_pos, jnp.exp(scores - logs_row[...]), 0.0)
            dweights = nt(keys[:, :latent], grads)
            dscores = (weights * (dweights - delta_row[...])).astype(BF)
            weights = weights.astype(BF)
            key_part = nn(dscores, queries) * score_scale
            value_part = nn(weights, grads)
            kp[at, :latent] = key_part[:, :latent] + value_part
            kp[at, latent:] = key_part[:, latent:]
            kp_b[at, :full] = kp[at, :].astype(BF)
            qacc[...] += tn(dscores, keys)
            for i in range(per // 2):
                q = m * (per // 2) + i

                @pl.when(q < chip + core)
                def _():
                    theirs = block_rows(2 * q + 1 - core)
                    to(kp_b.at[theirs, :], kpair_in.at[q], K_KPAIR, q, q, sib).start()

            return carry

        lax.fori_loop(0, last + 1, visit, 0)
        pending.append(lambda: each(0, chip + core, lambda q: sent(kpair_in.at[0], K_KPAIR, q)))
        q3[...] = (qacc[...] * score_scale).astype(BF).reshape(length, heads, full)
        start(q3, qg_out, O_QG)

    def sums_here():
        sums_here_of(pl.ds(0, 2), K_SUM)
        sums_here_of(pl.ds(2, 1), K_SUMD)

    def experts_step():
        def total_of(j):
            total = sum_in[0, j].astype(F32)
            for q in range(1, chips):
                total = total + sum_in[q, j].astype(F32)
            return total

        hidden, gate_delta, up_delta = expert_step(total_of(0), total_of(1), total_of(2))
        dl[core, chip, 0] = hidden
        dl[core, chip, 1] = gate_delta
        dl[core, chip, 2] = up_delta

    def send_deltas():
        gather_start(delta_block, K_DEL)
        gather_second(delta_block, K_DEL, first)
        here = delta_block(chip)
        to(here, here, K_DELF, chip, chip, sib).start()
        gather_pending(here, K_DEL, K_DELF)

    def key_pairs():
        def step(q):
            arrived(kpair_in.at[q], K_KPAIR, q)
            both = kp[block_rows(2 * q + core), :] + kpair_in[q, :, :full].astype(F32)
            ksum_out[q, :, :full] = both.astype(BF)

        each(0, chip + 1 - core, step)

        @pl.when(core == 1)
        def _():
            ksum_out[chip, :, :full] = kp[my_rows, :].astype(BF)

        def send(i):
            s, g = 1 + lax.div(i, side), lax.rem(i, side)
            f = turned(first, s)
            to(
                ksum_out.at[at(f, g)],
                ksum_in.at[first * side + g],
                K_KSUM,
                i,
                first * side + g,
                peer(at(f, second)),
            ).start()

        each(0, side * (side - 1), send)
        pending.append(
            lambda: each(0, side * (side - 1), lambda i: sent(ksum_out.at[0], K_KSUM, i))
        )

    def key_lines():
        def step(i):
            s, g = 1 + lax.div(i, side), lax.rem(i, side)
            f = turned(first, side - s)
            arrived(ksum_in.at[f * side + g], K_KSUM, f * side + g)

        each(0, side * (side - 1), step)

        def line(g):
            total = ksum_out[at(first, g), :, :full].astype(F32)
            for s in range(1, side):
                total = total + ksum_in[turned(first, s) * side + g, :, :full].astype(F32)
            return total

        def send(s):
            g = turned(second, s)
            kcol_out[s, :, :full] = line(g).astype(BF)
            to(
                kcol_out.at[s], kcol_in.at[second], K_KCOL, s, second, peer(at(first, g))
            ).start()

        each(1, side, send)
        zpart[...] = line(second)
        pending.append(lambda: each(1, side, lambda s: sent(kcol_out.at[0], K_KCOL, s)))

    def pass_deltas():
        gather_first_rest(delta_block, K_DEL, K_DELF)

    def pass_deltas_on():
        gather_second_rest(delta_block, K_DEL, K_DELF)

    def deltas_here():
        each(0, chips, lambda q: arrived(dl.at[1 - core, q], K_DELF, q))

    def delta_of(h, j):
        return dl[h, :, j].reshape(chips * blk, half)

    def go_back():
        back = jnp.zeros((groups * blk, width), F32)
        for h in range(2):
            cols = slice(h * half, (h + 1) * half)
            back = back + nt(delta_of(h, 1), wg[:, cols]) + nt(delta_of(h, 2), wu[:, cols])
        back_out[:, :width] = back.astype(BF)

        def step(s):
            zz = ahead(s)
            to(back_out.at[line_rows(zz), :], ret.at[mine, :], K_BACK, s, z, (c, zz)).start()

        each(1, groups, step)
        ret[mine, :] = back_out[mine, :]
        pending.append(lambda: each(1, groups, lambda s: sent(back_out.at[mine, :], K_BACK, s)))

    def key_sums():
        def step(s):
            g = turned(second, s)
            arrived(kcol_in.at[g], K_KCOL, g)
            zpart[...] += kcol_in[g, :, :full].astype(F32)

        each(1, side, step)
        zfin[:, :full] = zpart[...].astype(BF)

        def send_share(i):
            @pl.when(owner_z(i) != z)
            def _():
                to(
                    zfin.at[share_rows(i), :], zsum_in.at[z], K_ZSUM, i, z, (c, owner_z(i))
                ).start()

        each(0, owners, send_share)

        def share_sent(i):
            @pl.when(owner_z(i) != z)
            def _():
                sent(zfin.at[share_rows(0), :], K_ZSUM, i)

        pending.append(lambda: each(0, owners, share_sent))

    def weight_grads():
        for h in range(2):
            cols = slice(h * half, (h + 1) * half)
            gg[:, cols] = tn(arr[0, :, :width], delta_of(h, 1)).astype(BF)
            ug[:, cols] = tn(arr[0, :, :width], delta_of(h, 2)).astype(BF)
            dg[:, cols] = tn(arr[1, :, :width], delta_of(h, 0)).astype(BF)
        start(gg, gg_out, O_GG)
        start(ug, ug_out, O_UG)
        start(dg, dg_out, O_DG)

    def share_sums():
        @pl.when(is_owner)
        def _():
            def shares_here(s):
                zz = ahead(s)
                arrived(zsum_in.at[zz], K_ZSUM, zz)

            each(1, groups, shares_here)
            zsum_in[z] = zfin[share_rows(mine_share), :]
            total = zsum_in[0, :, :full].astype(F32)
            for zz in range(1, groups):
                total = total + zsum_in[zz, :, :full].astype(F32)
            zout[share_rows(mine_share), :full] = total.astype(BF)

            def send_rows(s):
                zz = ahead(s)
                there = zout.at[share_rows(mine_share), :]
                to(there, there, K_ZOUT, s, mine_share, (c, zz)).start()

            each(1, groups, send_rows)

        def rows_sent():
            @pl.when(is_owner)
            def _():
                each(1, groups, lambda s: sent(zfin.at[share_rows(0), :], K_ZOUT, s))

        pending.append(rows_sent)

    def back_here():
        def step(s):
            zz = behind(s)
            arrived(ret.at[line_rows(zz), :], K_BACK, zz)

        each(1, groups, step)
        igt[...] = tn(ret[:, :width], place[...]).astype(BF)
        start(igt, ig_out, O_IG)

    def rows_here():
        def step(i):
            @pl.when(owner_z(i) != z)
            def _():
                arrived(zout.at[share_rows(i), :], K_ZOUT, i)

        each(0, owners, step)
        lgt[...] = zout[:, :full]
        start(lgt, lg_out, O_LG)

    def finish():
        for wait in pending:
            wait()
        ready(*list(copies))

    for phase in (
        load,
        greet,
        dispatch,
        met,
        send_inputs,
        send_latents,
        send_grads,
        row_values,
        pass_latents,
        pass_latents_on,
        project_inputs,
        send_input_sums,
        latents_here,
        attention,
        project_grads,
        send_grad_sums,
        key_pairs,
        sums_here,
        experts_step,
        send_deltas,
        key_lines,
        pass_deltas,
        key_sums,
        pass_deltas_on,
        deltas_here,
        go_back,
        weight_grads,
        share_sums,
        back_here,
        rows_here,
        finish,
    ):
        phase()


def hand_out(count, *refs):
    stages, sems = refs[2 * count : 3 * count], refs[3 * count]
    ins = [pltpu.make_async_copy(refs[i], stages[i], sems.at[i]) for i in range(count)]
    outs = [
        pltpu.make_async_copy(stages[i], refs[count + i], sems.at[count + i])
        for i in range(count)
    ]
    for copy in ins:
        copy.start()
    for i in range(count):
        ins[i].wait()
        outs[i].start()
    for copy in outs:
        copy.wait()


def shards(
    chips,
    groups,
    queries,
    out_grad,
    attn_out,
    log_totals,
    latents,
    moe_inputs,
    moe_grad,
    expert_ids,
    gate_weight,
    up_weight,
    down_weight,
):
    length, heads, full = queries.shape
    latent = out_grad.shape[2]
    rows = length * heads
    tokens, width = moe_inputs.shape
    hidden = gate_weight.shape[2]
    half = hidden // 2
    blk = 16
    slots = groups * blk
    keys = length * chips * 2
    side = math.isqrt(chips)
    hbm = pl.BlockSpec(memory_space=pltpu.HBM)
    anywhere = pl.BlockSpec(memory_space=pl.ANY)
    lanes = max(chips + side, groups)
    owners = min(4, groups)
    weight = (width, hidden)
    wide = -(-width // 128) * 128
    padded = -(-full // 128) * 128
    results = (
        jax.ShapeDtypeStruct((length, heads, full), BF),
        jax.ShapeDtypeStruct((length, full), BF),
        jax.ShapeDtypeStruct((width, tokens), BF),
        jax.ShapeDtypeStruct(weight, BF),
        jax.ShapeDtypeStruct(weight, BF),
        jax.ShapeDtypeStruct(weight, BF),
    )
    held = pl.pallas_call(
        functools.partial(body, chips, side, groups),
        out_shape=results,
        in_specs=[hbm] * 11,
        out_specs=(anywhere,) * 6,
        scratch_shapes=[
            pltpu.VMEM((length, heads, full), BF),
            pltpu.VMEM((length, heads, latent), BF),
            pltpu.VMEM((length, heads, latent), BF),
            pltpu.VMEM((heads, length), BF),
            pltpu.VMEM((1, tokens), jnp.int32),
            pltpu.VMEM((width, tokens), BF),
            pltpu.VMEM((width, tokens), BF),
            pltpu.VMEM(weight, BF),
            pltpu.VMEM(weight, BF),
            pltpu.VMEM(weight, BF),
            pltpu.VMEM((rows, full), BF),
            pltpu.VMEM((rows, latent), BF),
            pltpu.VMEM((1, rows), F32),
            pltpu.VMEM((1, rows), F32),
            pltpu.VMEM((slots, tokens), BF),
            pltpu.VMEM((2, slots, wide), BF),
            pltpu.VMEM((2, slots, wide), BF),
            pltpu.VMEM((3, slots, half), F32),
            pltpu.VMEM((3, slots, half), F32),
            pltpu.VMEM((3, slots, half), F32),
            pltpu.VMEM((chips, 3, blk, half), BF),
            pltpu.VMEM((chips, 3, blk, half), BF),
            pltpu.VMEM((2, chips, 3, blk, half), BF),
            pltpu.VMEM((slots, wide), BF),
            pltpu.VMEM((slots, wide), BF),
            pltpu.VMEM((keys, padded), BF),
            pltpu.VMEM((rows, full), F32),
            pltpu.VMEM((keys, full), F32),
            pltpu.VMEM((keys, padded), BF),
            pltpu.VMEM((chips, length, padded), BF),
            pltpu.VMEM((chips, length, padded), BF),
            pltpu.VMEM((chips, length, padded), BF),
            pltpu.VMEM((side, length, padded), BF),
            pltpu.VMEM((side, length, padded), BF),
            pltpu.VMEM((length, full), F32),
            pltpu.VMEM((groups, length // owners, padded), BF),
            pltpu.VMEM((length, padded), BF),
            pltpu.VMEM((length, padded), BF),
            pltpu.VMEM((width, tokens), BF),
            pltpu.VMEM((length, full), BF),
            pltpu.VMEM((length, full), BF),
            pltpu.VMEM(weight, BF),
            pltpu.VMEM(weight, BF),
            pltpu.VMEM(weight, BF),
            pltpu.SemaphoreType.DMA((KINDS, lanes)),
            pltpu.SemaphoreType.DMA((KINDS, lanes)),
            pltpu.SemaphoreType.DMA((17,)),
        ],
        compiler_params=pltpu.CompilerParams(
            collective_id=0, has_side_effects=True, vmem_limit_bytes=VMEM
        ),
    )(
        queries,
        out_grad,
        attn_out,
        log_totals,
        latents,
        jnp.transpose(moe_inputs),
        jnp.transpose(moe_grad),
        expert_ids.reshape(1, tokens),
        gate_weight.reshape(weight),
        up_weight.reshape(weight),
        down_weight.reshape(weight),
    )
    qg, lg, ig, gg, ug, dg = pl.pallas_call(
        functools.partial(hand_out, 6),
        out_shape=results,
        in_specs=[anywhere] * 6,
        out_specs=(anywhere,) * 6,
        scratch_shapes=[pltpu.VMEM(r.shape, BF) for r in results]
        + [pltpu.SemaphoreType.DMA((12,))],
        compiler_params=pltpu.CompilerParams(vmem_limit_bytes=VMEM),
    )(*held)
    return (
        qg,
        lg,
        jnp.transpose(ig),
        gg.reshape((1,) + weight),
        ug.reshape((1,) + weight),
        dg.reshape((1,) + weight),
    )


def solution(mesh):
    chips = mesh.shape["ctx"] // 2
    groups = mesh.shape["exp"]
    return jax.shard_map(
        functools.partial(shards, chips, groups),
        mesh=mesh,
        in_specs=(
            P("ctx", "exp", None),
            P("ctx", "exp", None),
            P("ctx", "exp", None),
            P("exp", "ctx"),
            P("ctx", None),
            P("exp", "ctx"),
            P("exp", "ctx"),
            P("exp", None),
            P("exp", "ctx", None),
            P("exp", "ctx", None),
            P("exp", "ctx", None),
        ),
        out_specs=(
            P("ctx", "exp", None),
            P("ctx", None),
            P("exp", "ctx"),
            P("exp", "ctx", None),
            P("exp", "ctx", None),
            P("exp", "ctx", None),
        ),
        check_vma=False,
    )
```

time: 114 us -> 88.6 us (0.78)
  the two profiles are of different devices: /device:TPU:4 before, /device:TPU:1 now
where the time goes in v2:
time: 88.6 us; the launch traced here: 87.2 us
  Pallas kernels  86.6 us (98%)
    pallas_call x1, Pallas kernels, shards(): pl.pallas_call(functools.partial(body, chips, side, groups), out_shape=re...  84.2 us
    pallas_call x1, Pallas kernels, shards(): pl.pallas_call(functools.partial(hand_out, 6), out_shape=results, in_spec...  2.36 us

profile of v2, /device:TPU:1, one launch (start us, length us, event | category | flops | bytes accessed | tf_op | source)
XLA Modules:
  0.0 87.2 jit_solution(2202768030418224536)
XLA Ops:
  0.6 84.2 %shard_map.154 = (bf16[64,4,576]{2,1,0:T(4,128)(2,1)}, bf16[64,576]{1,0:T(8,128)(2,1)}, bf16[224,128]{1,0:T(8,128)(2,1)}, bf16[224,1024]{1,0:T(8,128)(2,1)}, bf1...) custom-call(bf16[64,4,576]{2,1,0:T(4,128)(2,1)} %q_in.1, bf16[64,4,512]{2,1,0:T(4,128)(2,1)} %g_in.1, ...), custom_call_target="tpu_custom_call" | custom-call | tf_op jit(solution)/shard_map/pallas_call | solution.py:777
  84.8 2.4 %shard_map.155 = (bf16[64,4,576]{2,1,0:T(4,128)(2,1)}, bf16[64,576]{1,0:T(8,128)(2,1)}, bf16[224,128]{1,0:T(8,128)(2,1)}, bf16[224,1024]{1,0:T(8,128)(2,1)}, bf1...) custom-call(bf16[64,4,576]{2,1,0:T(4,128)(2,1)} %get-tuple-element.18.refs_0_, ...), custom_call_target="tpu_custom_call" | custom-call | tf_op jit(solution)/shard_map/pallas_call | solution.py:847

commit v3 on v2

--- a/solution.py
+++ b/solution.py
@@ -24,14 +24,16 @@
     K_SUMD,
     K_DEL,
     K_DELF,
+    K_HID,
+    K_HIDF,
     K_BACK,
     K_KPAIR,
     K_KSUM,
     K_KCOL,
     K_ZSUM,
     K_ZOUT,
-) = range(15)
-KINDS = 15
+) = range(17)
+KINDS = 17
 (
     L_LAT,
     L_IDS,
@@ -159,7 +161,7 @@
     owners = min(4, groups)
     spacing = groups // owners
     share = length // owners
-    chunk = min(256, lat_all.shape[0])
+    chunk = min(512, lat_all.shape[0])
     per = chunk // length
     last = lax.div(c, per)
     here_y = lax.div(chip, side)
@@ -184,11 +186,14 @@
     def turned(v, s):
         return lax.rem(v + s, side)
 
+    def spread(s):
+        return groups // 2 + lax.div(s, 2) * (2 * lax.rem(s, 2) - 1)
+
     def ahead(s):
-        return lax.rem(z + s, groups)
+        return lax.rem(z + spread(s), groups)
 
     def behind(s):
-        return lax.rem(z + groups - s, groups)
+        return lax.rem(z + groups - spread(s), groups)
 
     def to(src, dst, kind, si, ri, dev):
         return pltpu.make_async_remote_copy(
@@ -280,9 +285,6 @@
 
     def lat_block(q):
         return lat_all.at[block_rows(2 * q + core), :]
-
-    def delta_block(q):
-        return dl.at[core, q]
 
     copies = {}
 
@@ -455,38 +457,48 @@
     def latents_here():
         each(0, chips, lambda q: arrived(lat_all.at[block_rows(2 * q + 1 - core), :], K_LATF, q))
 
+    def visit(m, carry):
+        at_rows = pl.ds(pl.multiple_of(m * chunk, chunk), chunk)
+        keys = lat_all[at_rows, :full]
+        queries = q_ref[...]
+        grads = g_ref[...]
+        scores = nt(keys, queries) * score_scale
+        key_pos = m * chunk + lax.broadcasted_iota(jnp.int32, (chunk, rows), 0)
+        query_pos = c * length + lax.broadcasted_iota(jnp.int32, (chunk, rows), 1) // heads
+        weights = jnp.where(key_pos <= query_pos, jnp.exp(scores - logs_row[...]), 0.0)
+        dweights = nt(keys[:, :latent], grads)
+        dscores = (weights * (dweights - delta_row[...])).astype(BF)
+        weights = weights.astype(BF)
+        key_part = nn(dscores, queries) * score_scale
+        value_part = nn(weights, grads)
+        kp[at_rows, :latent] = key_part[:, :latent] + value_part
+        kp[at_rows, latent:] = key_part[:, latent:]
+        kp_b[at_rows, :full] = kp[at_rows, :].astype(BF)
+        qacc[...] += tn(dscores, keys)
+        for i in range(per // 2):
+            q = m * (per // 2) + i
+
+            @pl.when(q < chip + core)
+            def _():
+                theirs = block_rows(2 * q + 1 - core)
+                to(kp_b.at[theirs, :], kpair_in.at[q], K_KPAIR, q, q, sib).start()
+
+        return carry
+
     def attention():
         qacc[...] = jnp.zeros_like(qacc)
-
-        def visit(m, carry):
-            at = pl.ds(pl.multiple_of(m * chunk, chunk), chunk)
-            keys = lat_all[at, :full]
-            queries = q_ref[...]
-            grads = g_ref[...]
-            scores = nt(keys, queries) * score_scale
-            key_pos = m * chunk + lax.broadcasted_iota(jnp.int32, (chunk, rows), 0)
-            query_pos = c * length + lax.broadcasted_iota(jnp.int32, (chunk, rows), 1) // heads
-            weights = jnp.where(key_pos <= query_pos, jnp.exp(scores - logs_row[...]), 0.0)
-            dweights = nt(keys[:, :latent], grads)
-            dscores = (weights * (dweights - delta_row[...])).astype(BF)
-            weights = weights.astype(BF)
-            key_part = nn(dscores, queries) * score_scale
-            value_part = nn(weights, grads)
-            kp[at, :latent] = key_part[:, :latent] + value_part
-            kp[at, latent:] = key_part[:, latent:]
-            kp_b[at, :full] = kp[at, :].astype(BF)
-            qacc[...] += tn(dscores, keys)
-            for i in range(per // 2):
-                q = m * (per // 2) + i
-
-                @pl.when(q < chip + core)
-                def _():
-                    theirs = block_rows(2 * q + 1 - core)
-                    to(kp_b.at[theirs, :], kpair_in.at[q], K_KPAIR, q, q, sib).start()
-
-            return carry
-
         lax.fori_loop(0, last + 1, visit, 0)
+        attention_end()
+
+    def attention_some():
+        qacc[...] = jnp.zeros_like(qacc)
+        lax.fori_loop(0, lax.div(last + 1, 2), visit, 0)
+
+    def attention_rest():
+        lax.fori_loop(lax.div(last + 1, 2), last + 1, visit, 0)
+        attention_end()
+
+    def attention_end():
         pending.append(lambda: each(0, chip + core, lambda q: sent(kpair_in.at[0], K_KPAIR, q)))
         q3[...] = (qacc[...] * score_scale).astype(BF).reshape(length, heads, full)
         start(q3, qg_out, O_QG)
@@ -507,12 +519,57 @@
         dl[core, chip, 1] = gate_delta
         dl[core, chip, 2] = up_delta
 
+    def deltas_of(q):
+        return dl.at[core, q, pl.ds(1, 2)]
+
+    def hidden_of(q):
+        return dl.at[core, q, pl.ds(0, 1)]
+
+    def all_of(q):
+        return dl.at[core, q]
+
+    def send_blocks(block, kind, fkind):
+        gather_start(block, kind)
+        gather_second(block, kind, first)
+        here = block(chip)
+        to(here, here, fkind, chip, chip, sib).start()
+        gather_pending(here, kind, fkind)
+
+    def send_all():
+        send_blocks(all_of, K_DEL, K_DELF)
+
+    def pass_all():
+        gather_first_rest(all_of, K_DEL, K_DELF)
+
+    def pass_all_on():
+        gather_second_rest(all_of, K_DEL, K_DELF)
+
+    def all_here():
+        each(0, chips, lambda q: arrived(dl.at[1 - core, q], K_DELF, q))
+
     def send_deltas():
-        gather_start(delta_block, K_DEL)
-        gather_second(delta_block, K_DEL, first)
-        here = delta_block(chip)
-        to(here, here, K_DELF, chip, chip, sib).start()
-        gather_pending(here, K_DEL, K_DELF)
+        send_blocks(deltas_of, K_DEL, K_DELF)
+
+    def pass_deltas():
+        gather_first_rest(deltas_of, K_DEL, K_DELF)
+
+    def pass_deltas_on():
+        gather_second_rest(deltas_of, K_DEL, K_DELF)
+
+    def deltas_here():
+        each(0, chips, lambda q: arrived(dl.at[1 - core, q, pl.ds(1, 2)], K_DELF, q))
+
+    def send_hidden():
+        send_blocks(hidden_of, K_HID, K_HIDF)
+
+    def pass_hidden():
+        gather_first_rest(hidden_of, K_HID, K_HIDF)
+
+    def pass_hidden_on():
+        gather_second_rest(hidden_of, K_HID, K_HIDF)
+
+    def hidden_here():
+        each(0, chips, lambda q: arrived(dl.at[1 - core, q, pl.ds(0, 1)], K_HIDF, q))
 
     def key_pairs():
         def step(q):
@@ -568,15 +625,6 @@
         zpart[...] = line(second)
         pending.append(lambda: each(1, side, lambda s: sent(kcol_out.at[0], K_KCOL, s)))
 
-    def pass_deltas():
-        gather_first_rest(delta_block, K_DEL, K_DELF)
-
-    def pass_deltas_on():
-        gather_second_rest(delta_block, K_DEL, K_DELF)
-
-    def deltas_here():
-        each(0, chips, lambda q: arrived(dl.at[1 - core, q], K_DELF, q))
-
     def delta_of(h, j):
         return dl[h, :, j].reshape(chips * blk, half)
 
@@ -625,9 +673,13 @@
             cols = slice(h * half, (h + 1) * half)
             gg[:, cols] = tn(arr[0, :, :width], delta_of(h, 1)).astype(BF)
             ug[:, cols] = tn(arr[0, :, :width], delta_of(h, 2)).astype(BF)
-            dg[:, cols] = tn(arr[1, :, :width], delta_of(h, 0)).astype(BF)
         start(gg, gg_out, O_GG)
         start(ug, ug_out, O_UG)
+
+    def down_grads():
+        for h in range(2):
+            cols = slice(h * half, (h + 1) * half)
+            dg[:, cols] = tn(arr[1, :, :width], delta_of(h, 0)).astype(BF)
         start(dg, dg_out, O_DG)
 
     def share_sums():
@@ -686,30 +738,32 @@
         load,
         greet,
         dispatch,
+        row_values,
         met,
         send_inputs,
         send_latents,
         send_grads,
-        row_values,
         pass_latents,
         pass_latents_on,
         project_inputs,
         send_input_sums,
         latents_here,
-        attention,
+        attention_some,
         project_grads,
         send_grad_sums,
+        attention_rest,
         key_pairs,
         sums_here,
         experts_step,
-        send_deltas,
+        send_all,
         key_lines,
-        pass_deltas,
+        pass_all,
         key_sums,
-        pass_deltas_on,
-        deltas_here,
+        pass_all_on,
+        all_here,
         go_back,
         weight_grads,
+        down_grads,
         share_sums,
         back_here,
         rows_here,

time: 88.6 us -> 84.8 us (0.957); the launches traced: 87.2 us -> 84.6 us
  Pallas kernels: 86.6 us -> 83.9 us
    pallas_call x1, Pallas kernels: 84.2 us -> 81.6 us  [shards(): pl.pallas_call(functools.partial(body, chips, side, groups), out_shape=re...]
where the time goes in v3:
time: 84.8 us; the launch traced here: 84.6 us
  Pallas kernels  83.9 us (99%)
    pallas_call x1, Pallas kernels, shards(): pl.pallas_call(functools.partial(body, chips, side, groups), out_shape=re...  81.6 us
    pallas_call x1, Pallas kernels, shards(): pl.pallas_call(functools.partial(hand_out, 6), out_shape=results, in_spec...  2.36 us

profile of v3, /device:TPU:1, one launch (start us, length us, event | category | flops | bytes accessed | tf_op | source)
XLA Modules:
  0.0 84.6 jit_solution(4323052823184222224)
XLA Ops:
  0.6 81.6 %shard_map.154 = (bf16[64,4,576]{2,1,0:T(4,128)(2,1)}, bf16[64,576]{1,0:T(8,128)(2,1)}, bf16[224,128]{1,0:T(8,128)(2,1)}, bf16[224,1024]{1,0:T(8,128)(2,1)}, bf1...) custom-call(bf16[64,4,576]{2,1,0:T(4,128)(2,1)} %q_in.1, bf16[64,4,512]{2,1,0:T(4,128)(2,1)} %g_in.1, ...), custom_call_target="tpu_custom_call" | custom-call | tf_op jit(solution)/shard_map/pallas_call | solution.py:831
  82.2 2.4 %shard_map.155 = (bf16[64,4,576]{2,1,0:T(4,128)(2,1)}, bf16[64,576]{1,0:T(8,128)(2,1)}, bf16[224,128]{1,0:T(8,128)(2,1)}, bf16[224,1024]{1,0:T(8,128)(2,1)}, bf1...) custom-call(bf16[64,4,576]{2,1,0:T(4,128)(2,1)} %get-tuple-element.18.refs_0_, ...), custom_call_target="tpu_custom_call" | custom-call | tf_op jit(solution)/shard_map/pallas_call | solution.py:901

commit v4 on v3

--- a/solution.py
+++ b/solution.py
@@ -299,6 +299,9 @@
     pending = []
 
     def load():
+        lat_all[pl.ds(pl.multiple_of(last * chunk, chunk), chunk), :] = jnp.zeros(
+            (chunk, lat_all.shape[1]), BF
+        )
         ksum_out[...] = jnp.zeros_like(ksum_out)
         start(ids_in, ids, L_IDS)
         start(x_in, xt, L_X)
@@ -361,19 +364,85 @@
     def send_grads():
         send_tokens_of(1, K_TOKG)
 
+    def to_first(b, r):
+        passed = jnp.logical_and(core == 0, lax.div(b, side) < side - 1)
+        return jnp.logical_or(b < r, passed)
+
+    def latents_first(act):
+        def step(s):
+            r = at(turned(first, s), second)
+
+            @pl.when(to_first(chip, r))
+            def _():
+                act(chip, K_LAT, s, r)
+
+        each(1, side, step)
+
+    def latents_second(f, act):
+        held = at(f, second)
+
+        def step(s):
+            r = at(first, turned(second, s))
+
+            @pl.when(held < r)
+            def _():
+                act(held, K_LAT, side * (1 + lax.rem(f - first + side, side)) + s, r)
+
+        each(1, side, step)
+
+    def send_block(q, kind, si, r):
+        to(lat_block(q), lat_block(q), kind, si, q, peer(r)).start()
+
+    def block_sent(q, kind, si, r):
+        sent(my_block, kind, si)
+
+    def latent_forward(q):
+        to(lat_block(q), lat_block(q), K_LATF, q, q, sib).start()
+
     def send_latents():
         ready(L_LAT)
         lat_all[my_rows, :full] = lat_own[...]
-        gather_start(lat_block, K_LAT)
-        gather_second(lat_block, K_LAT, first)
-        to(my_block, my_block, K_LATF, chip, chip, sib).start()
-        gather_pending(my_block, K_LAT, K_LATF)
+        latents_first(send_block)
+        latents_second(first, send_block)
+        latent_forward(chip)
+        pending.append(lambda: latents_first(block_sent))
+        pending.append(lambda: latents_second(first, block_sent))
+        pending.append(lambda: each(0, chip + 1, lambda q: sent(my_block, K_LATF, q)))
+
+    def first_latents(get, act):
+        def step(s):
+            f = turned(first, side - s)
+            q = at(f, second)
+
+            @pl.when(to_first(q, chip))
+            def _():
+                get(q)
+                latents_second(f, act)
+
+        each(1, side, step)
 
     def pass_latents():
-        gather_first_rest(lat_block, K_LAT, K_LATF)
+        def get(q):
+            arrived(lat_block(q), K_LAT, q)
+
+            @pl.when(q < chip)
+            def _():
+                latent_forward(q)
+
+        first_latents(get, send_block)
+        pending.append(lambda: first_latents(lambda q: None, block_sent))
 
     def pass_latents_on():
-        gather_second_rest(lat_block, K_LAT, K_LATF)
+        def step(i):
+            f = turned(first, side - lax.rem(i, side))
+            q = at(f, turned(second, side - lax.div(i, side)))
+
+            @pl.when(q < chip)
+            def _():
+                arrived(lat_block(q), K_LAT, q)
+                latent_forward(q)
+
+        each(side, chips, step)
 
     def row_values():
         ready(L_Q, L_G, L_A, L_LOG)
@@ -455,7 +524,9 @@
         send_sums_of(pl.ds(2, 1), K_SUMD)
 
     def latents_here():
-        each(0, chips, lambda q: arrived(lat_all.at[block_rows(2 * q + 1 - core), :], K_LATF, q))
+        each(
+            0, chip + 1, lambda q: arrived(lat_all.at[block_rows(2 * q + 1 - core), :], K_LATF, q)
+        )
 
     def visit(m, carry):
         at_rows = pl.ds(pl.multiple_of(m * chunk, chunk), chunk)

time: 84.8 us -> 84.9 us (level)
  no operation moved by 1% of the time
where the time goes in v4:
time: 84.9 us; the launch traced here: 84.7 us
  Pallas kernels  84.1 us (99%)
    pallas_call x1, Pallas kernels, shards(): pl.pallas_call(functools.partial(body, chips, side, groups), out_shape=re...  81.7 us
    pallas_call x1, Pallas kernels, shards(): pl.pallas_call(functools.partial(hand_out, 6), out_shape=results, in_spec...  2.36 us

profile of v4, /device:TPU:1, one launch (start us, length us, event | category | flops | bytes accessed | tf_op | source)
XLA Modules:
  0.0 84.7 jit_solution(758142226395729617)
XLA Ops:
  0.6 81.7 %shard_map.154 = (bf16[64,4,576]{2,1,0:T(4,128)(2,1)}, bf16[64,576]{1,0:T(8,128)(2,1)}, bf16[224,128]{1,0:T(8,128)(2,1)}, bf16[224,1024]{1,0:T(8,128)(2,1)}, bf1...) custom-call(bf16[64,4,576]{2,1,0:T(4,128)(2,1)} %q_in.1, bf16[64,4,512]{2,1,0:T(4,128)(2,1)} %g_in.1, ...), custom_call_target="tpu_custom_call" | custom-call | tf_op jit(solution)/shard_map/pallas_call | solution.py:902
  82.3 2.4 %shard_map.155 = (bf16[64,4,576]{2,1,0:T(4,128)(2,1)}, bf16[64,576]{1,0:T(8,128)(2,1)}, bf16[224,128]{1,0:T(8,128)(2,1)}, bf16[224,1024]{1,0:T(8,128)(2,1)}, bf1...) custom-call(bf16[64,4,576]{2,1,0:T(4,128)(2,1)} %get-tuple-element.18.refs_0_, ...), custom_call_target="tpu_custom_call" | custom-call | tf_op jit(solution)/shard_map/pallas_call | solution.py:972
